TPU v7x, 32 devices: a whole 2x2x4 slice. The times are simulated.
32 devices in a mesh: pts: 8 (over z, x), orb: 4 (over y, core).
Axes of the slice: x: 2, y: 2, z: 4, core: 2. Of those that a mesh axis runs over, the one named last changes fastest.
Arguments:
- occ_points: float32 [20480, 1024], P('pts', 'orb'), may hold values from -0.1875 to 0.1875
- vir_points: float32 [20480, 9216], P('pts', 'orb'), may hold values from -0.0625 to 0.0625
- occ_cols: float32 [256, 1024], P('pts', 'orb'), may hold values from -6 to 6
- vir_cols: float32 [256, 9216], P('pts', 'orb'), may hold values from -6 to 6
- occ_energy: float32 [1024], P('orb'), may hold values from -1.5 to -0.2
- vir_energy: float32 [9216], P('orb'), may hold values from 0.2 to 3
- plane_waves: float32 [8192, 20480], P('orb', 'pts'), may hold values from -0.0390625 to 0.0390625
Outputs:
- projected: float32 [2, 8192, 256], P(None, 'orb', 'pts')
All inputs are finite; a program needn't handle non-finite values.
Results may differ from a plain program's by a relative error of at most 0.00011.
Values sent between devices are 32-bit elements; how exact they have to be, the bound alone decides.
A program may use at most 128 MiB of HBM per device.

v0:
```python
import jax
import jax.numpy as jnp
from jax import lax
from jax.sharding import PartitionSpec as P

IMAG_TIMES = (0.3, 1.2)
FREQUENCIES = (0.5, 2.0)
QUAD_WEIGHTS = (0.6, 1.8)


def make_table():
    moments = jnp.array(IMAG_TIMES, jnp.float32)
    omegas = jnp.array(FREQUENCIES, jnp.float32)
    weights = jnp.array(QUAD_WEIGHTS, jnp.float32)
    return 2.0 * weights[None, :] * jnp.cos(omegas[:, None] * moments[None, :])


def contract(left, right):
    return lax.dot_general(
        left,
        right,
        (((1,), (1,)), ((), ())),
        precision=lax.Precision.HIGHEST,
        preferred_element_type=jnp.float32,
    )


def on_device(occ_points, vir_points, occ_cols, vir_cols, occ_energy, vir_energy, plane_waves):
    occ_all, vir_all = (
        lax.all_gather(occ_cols, "pts", axis=0, tiled=True),
        lax.all_gather(vir_cols, "pts", axis=0, tiled=True),
    )
    row_count = occ_points.shape[0]
    columns = occ_all.shape[0]
    col_block = columns // lax.axis_size("orb")
    col_start = lax.axis_index("orb") * col_block
    moments = jnp.array(IMAG_TIMES, jnp.float32)
    occ_weight = jnp.exp(moments[:, None] * occ_energy[None, :])
    vir_weight = jnp.exp(-moments[:, None] * vir_energy[None, :])
    vir_scaled = (vir_all[None, :, :] * vir_weight[:, None, :]).reshape(2 * columns, -1)
    vir_green = contract(vir_points, vir_scaled).reshape(row_count, 2, columns)
    occ_scaled = (occ_all[None, :, :] * occ_weight[:, None, :]).reshape(2 * columns, -1)
    occ_rows, occ_whole = (
        lax.all_gather(occ_points, "orb", axis=1, tiled=True),
        lax.all_gather(occ_scaled, "orb", axis=1, tiled=True),
    )
    occ_whole = occ_whole.reshape(2, columns, -1)
    occ_block = lax.dynamic_slice_in_dim(occ_whole, col_start, col_block, 1).reshape(
        2 * col_block, -1
    )
    occ_green = contract(occ_rows, occ_block).reshape(row_count, 2, col_block)
    vir_green = lax.psum_scatter(vir_green, "orb", scatter_dimension=2, tiled=True)
    response = -(occ_green * vir_green)
    spectral = jnp.einsum("kt,rtc->rkc", make_table(), response, precision=lax.Precision.HIGHEST)
    spectral = lax.all_gather(spectral, "orb", axis=2, tiled=True)
    partial_value = jnp.dot(
        plane_waves,
        spectral.reshape(row_count, 2 * columns),
        precision=lax.Precision.HIGHEST,
        preferred_element_type=jnp.float32,
    )
    partial_value = partial_value.reshape(plane_waves.shape[0], 2, columns)
    summed = lax.psum_scatter(partial_value, "pts", scatter_dimension=2, tiled=True)
    return jnp.transpose(summed, (1, 0, 2))


def solution(mesh):
    in_specs = (
        P("pts", "orb"),
        P("pts", "orb"),
        P("pts", "orb"),
        P("pts", "orb"),
        P("orb"),
        P("orb"),
        P("orb", "pts"),
    )
    out_specs = P(None, "orb", "pts")
    return jax.shard_map(
        on_device, mesh=mesh, in_specs=in_specs, out_specs=out_specs, check_vma=False
    )
```

profile of v0, /device:TPU:0, one launch (start us, length us, event | category | flops | bytes accessed | tf_op | source)
XLA Modules:
  0.0 450.3 jit_solution(13105141568110135807)
XLA Ops:
  6.5 0.0 all-gather.9.cloned.1.call-start
  6.5 0.7 all-gather.9.cloned.1.call-update
  7.3 0.0 all-gather.5.cloned.1.call-start
  7.3 32.9 %all_gather.15 = f32[256,256]{1,0:T(8,128)S(1)} all-gather(f32[32,256]{1,0:T(8,128)} %param.13), channel_id=1, replica_groups=mesh['pts'=8,'orb'=4] {'pts'}, dimensions={0}, use_global_device_ids=true | all-gather | bytes 294912 | tf_op jit(solution)/shard_map/all_gather | solution.py:30
  40.2 0.8 multiply_exponential_fusion.1
  41.0 0.8 broadcast_multiply_fusion.1
  41.8 0.0 all-gather.5.cloned.1.call-update
  41.8 0.0 all-gather.7.cloned.1.call-start
  41.9 0.7 all-gather.7.cloned.1.call-update
  42.6 0.0 all-reduce.3.cloned.1.call-start
  42.6 0.8 multiply_exponential_fusion
  43.4 21.6 %all-gather.9.cloned.1.call-done = f32[256,2304]{1,0:T(8,128)} async-done(((f32[32,2304]{1,0:T(8,128)}), f32[256,2304]{1,0:T(8,128)}) %all-gather.9.cloned.1.call-update) | async-done | bytes 2359312 | tf_op jit(solution)/shard_map/all_gather | solution.py:31
  65.0 2.0 broadcast_multiply_fusion
  67.0 41.5 %fusion.12 = f32[512,2560]{1,0:T(8,128)S(1)} fusion(f32[512,2304]{1,0:T(8,128)S(1)} %bitcast.29, f32[2560,2304]{1,0:T(8,128)} %param.12), kind=kOutput, calls=%fused_computation.18 | convolution fusion | flops 36238786560 | bytes 33554432 | tf_op jit(solution)/shard_map/dot_general | solution.py:19
  108.5 6.3 %copy.17 = f32[2560,2,256]{0,1,2:T(2,128)} copy(f32[2560,2,256]{0,2,1:T(8,128)S(1)} %bitcast.27) | data formatting | bytes 10485760 | tf_op jit(solution)/shard_map/reshape | solution.py:41
  114.8 0.0 copy-start.1
  114.8 0.0 all-reduce.3.cloned.1.call-update
  114.9 0.0 all-gather.11.cloned.1.call-start
  114.9 0.6 copy-done.1
  115.5 0.6 dynamic-slice
  116.7 0.0 all-gather.5.cloned.1.call-done
  116.8 1.1 constant_dynamic-slice_fusion
  117.9 41.7 %all-gather.7.cloned.1.call-done = f32[2560,1024]{1,0:T(8,128)} async-done(((f32[2560,256]{1,0:T(8,128)}), f32[2560,1024]{1,0:T(8,128)}) %all-gather.7.cloned.1.call-update) | async-done | bytes 10485776 | tf_op jit(solution)/shard_map/all_gather | solution.py:44
  159.5 0.0 copy-start
  159.5 0.0 copy-start.2
  159.5 0.0 copy-start.3
  159.5 13.4 %fusion.11 = f32[128,2560]{1,0:T(8,128)S(1)} fusion(f32[128,1024]{1,0:T(8,128)S(1)} %bitcast.31, f32[2560,1024]{1,0:T(8,128)} %all-gather.7.cloned.1.call-done), kind=kOutput, calls=%fused_computation.17 | convolution fusion | flops 4026531840 | bytes 12320768 | tf_op jit(solution)/shard_map/dot_general | solution.py:19
  172.9 91.4 %all-reduce.3.cloned.1.call-done = f32[2560,2,256]{0,1,2:T(2,128)} async-done(((f32[2560,2,256]{0,1,2:T(2,128)}), f32[2560,2,256]{0,1,2:T(2,128)}) %all-reduce.3.cloned.1.call-update) | async-done | bytes 5242896
  264.3 0.0 copy-done
  264.3 0.0 copy-done.2
  264.4 0.0 copy-done.3
  264.4 7.9 %convolution_bitcast_fusion = f32[2560,2,64]{0,1,2:T(2,128)} fusion(f32[2560,2,256]{0,1,2:T(2,128)} %all-reduce.3.cloned.1.call-done, u32[]{:T(128)S(6)} %multiply.1, f32[2560,2,64]{0,2,1:T(8,128)S(1)} %bitcast.33, f32[2]{0:T(128)S(1)} %copy-done, f32[2]{0:T(128)S(1)} %copy-done.2, f32[2]{0:T(128)S(1)} %copy-done.3), kind=kOutput, calls=%fused_computation | convolution fusion | flops 8519688 | bytes 3932188 | tf_op jit(solution)/shard_map/kt,rtc->rkc/dot_general | solution.py:54
  272.2 0.0 all-gather.11.cloned.1.call-update
  272.2 0.0 reduce-scatter.2.cloned.1.call-start
  272.3 40.7 %all-gather.11.cloned.1.call-done = f32[2560,2,256]{0,1,2:T(2,128)} async-done(((f32[2560,2,64]{0,1,2:T(2,128)}), f32[2560,2,256]{0,1,2:T(2,128)}) %all-gather.11.cloned.1.call-update) | async-done | bytes 5242896 | tf_op jit(solution)/shard_map/all_gather | solution.py:55
  313.0 3.5 copy.19
  316.5 38.3 %fusion.13 = f32[512,2048]{1,0:T(8,128)} fusion(f32[2560,512]{0,1:T(8,128)S(1)} %bitcast.28, f32[2048,2560]{1,0:T(8,128)} %param.17), kind=kOutput, calls=%fused_computation.19 | convolution fusion | flops 32212254720 | bytes 30408704 | tf_op jit(solution)/shard_map/dot_general | solution.py:56
  354.8 0.0 reduce-scatter.2.cloned.1.call-update
  354.8 88.6 %reduce-scatter.2.cloned.1.call-done = f32[2048,2,32]{0,2,1:T(8,128)} async-done(((f32[2048,2,256]{0,2,1:T(8,128)}), f32[2048,2,32]{0,2,1:T(8,128)}) %reduce-scatter.2.cloned.1.call-update) | async-done | bytes 524304 | tf_op jit(solution)/shard_map/reduce_scatter | solution.py:63
Async XLA Ops:
  6.5 58.5 %all-gather.9.cloned.1.call-start = ((), (), s32[]{:S(2)}) async-start(), calls=%async_computation.3 | async-start | bytes 2654208 | tf_op jit(solution)/shard_map/all_gather | solution.py:31
  7.3 109.5 %all-gather.5.cloned.1.call-start = ((), (), s32[]{:S(2)}) async-start(), calls=%async_computation.1 | async-start | bytes 2621440 | tf_op jit(solution)/shard_map/all_gather | solution.py:45
  41.8 117.7 %all-gather.7.cloned.1.call-start = ((), (), s32[]{:S(2)}) async-start(), calls=%async_computation.2 | async-start | bytes 13107200 | tf_op jit(solution)/shard_map/all_gather | solution.py:44
  42.6 221.8 %all-reduce.3.cloned.1.call-start = ((), (), s32[]{:S(2)}) async-start(), calls=%async_computation.6 | async-start | bytes 10485760
  114.8 0.7 copy-start.1
  114.9 198.1 %all-gather.11.cloned.1.call-start = ((), (), s32[]{:S(2)}) async-start(), calls=%async_computation.4 | async-start | bytes 6553600 | tf_op jit(solution)/shard_map/all_gather | solution.py:55
  159.5 104.8 %copy-start = (f32[2]{0:T(128)S(1)}, f32[2]{0:T(128)}, u32[]{:S(2)}) copy-start(f32[2]{0:T(128)} %constant.18.clone) | copy-start | bytes 28
  159.5 104.8 %copy-start.2 = (f32[2]{0:T(128)S(1)}, f32[2]{0:T(128)}, u32[]{:S(2)}) copy-start(f32[2]{0:T(128)} %constant.19.clone) | copy-start | bytes 28
  159.5 104.8 %copy-start.3 = (f32[2]{0:T(128)S(1)}, f32[2]{0:T(128)}, u32[]{:S(2)}) copy-start(f32[2]{0:T(128)} %constant.22) | copy-start | bytes 28
  272.2 171.2 %reduce-scatter.2.cloned.1.call-start = ((), (), s32[]{:S(2)}) async-start(), calls=%async_computation.5 | async-start | bytes 4718592 | tf_op jit(solution)/shard_map/reduce_scatter | solution.py:63
Sparse Core Ops, SparseCore 0:
  9.5 55.4 all-gather.8
  66.6 21.1 all-gather.4
  89.3 70.1 all-gather.6
  161.8 102.5 all-reduce.2
  272.4 40.5 all-gather.10
  354.9 88.4 reduce-scatter.1
where the time goes:
time: 451 us; the launch traced here: 450 us
  waiting for transfers between devices  286 us (63%)
  matrix products  101 us (22%)
  blocking collectives  32.9 us (7%)
  between operations  14.2 us (3%)
  local copies, waits for them, and re-layouts  12.1 us (3%)
    unnamed x7, waiting for transfers between devices  92.9 us
    reduce_scatter x1, waiting for transfers between devices, on_device(): lax.psum_scatter(partial_value, 'pts', scatter_dimension=2, tiled=True)  88.6 us
    dot_general x2, matrix products, contract(): lax.dot_general(left, right, (((1,), (1,)), ((), ())), precision=lax.Prec...  54.9 us
    all_gather x1, waiting for transfers between devices, on_device(): lax.all_gather(occ_points, 'orb', axis=1, tiled=True)  41.7 us
    all_gather x1, waiting for transfers between devices, on_device(): spectral = lax.all_gather(spectral, 'orb', axis=2, tiled=True)  40.7 us
    dot_general x1, matrix products, on_device(): jnp.dot(plane_waves, spectral.reshape(row_count, 2 * columns), precision=...  38.3 us
    all_gather x1, blocking collectives, on_device(): lax.all_gather(occ_cols, 'pts', axis=0, tiled=True)  32.9 us
    all_gather x1, waiting for transfers between devices, on_device(): lax.all_gather(vir_cols, 'pts', axis=0, tiled=True)  21.6 us
  transfers between devices with their start and end apart: 6, of which 5 were waited for; matrix products, arithmetic and copies ran while one was open for 15% of the time, Pallas kernels for 0%

commit v1 on v0

v1 whole, which is shorter than its diff:
```python
import jax
import jax.numpy as jnp
from jax import lax
from jax.sharding import PartitionSpec as P

IMAG_TIMES = (0.3, 1.2)
FREQUENCIES = (0.5, 2.0)
QUAD_WEIGHTS = (0.6, 1.8)
G_SPLIT = 2


def make_table():
    moments = jnp.array(IMAG_TIMES, jnp.float32)
    omegas = jnp.array(FREQUENCIES, jnp.float32)
    weights = jnp.array(QUAD_WEIGHTS, jnp.float32)
    return 2.0 * weights[None, :] * jnp.cos(omegas[:, None] * moments[None, :])


def contract(left, right):
    return lax.dot_general(
        left,
        right,
        (((1,), (1,)), ((), ())),
        precision=lax.Precision.HIGH,
        preferred_element_type=jnp.float32,
    )


def swap(x, axis, bit):
    return lax.ppermute(x, axis, [(i, i ^ bit) for i in range(lax.axis_size(axis))])


def bits_of(count):
    width = count.bit_length() - 1
    return [1 << i for i in reversed(range(width))]


def masks_of(bits):
    masks = [0]
    for bit in bits:
        masks = masks + [m ^ bit for m in masks]
    return masks


def gather(x, axis, bits, dim):
    for bit in bits:
        x = jnp.concatenate([x, swap(x, axis, bit)], axis=dim)
    return x


def scatter_sum(x, axis, bits):
    for bit in reversed(bits):
        half = x.shape[0] // 2
        x = x[:half] + swap(x[half:], axis, bit)
    return x


def weighted(cols, weight):
    value = jnp.transpose(cols, (1, 0, 2, 3))[:, None] * weight[None, :, None, None, :]
    return value.reshape(-1, cols.shape[-1])


def on_device(occ_points, vir_points, occ_cols, vir_cols, occ_energy, vir_energy, plane_waves):
    pts_bits = bits_of(lax.axis_size("pts"))
    orb_bits = bits_of(lax.axis_size("orb"))
    outer, last = pts_bits[:-1], pts_bits[-1]
    orb = lax.axis_index("orb")
    orbs = lax.axis_size("orb")
    orb_masks = masks_of(orb_bits)
    rows = occ_points.shape[0]
    block = occ_cols.shape[0] // orbs
    table = make_table()
    moments = jnp.array(IMAG_TIMES, jnp.float32)
    occ_weight = jnp.exp(moments[:, None] * occ_energy[None, :])
    vir_weight = jnp.exp(-moments[:, None] * vir_energy[None, :])

    def relative(cols):
        cols = cols.reshape(orbs, block, -1)
        parts = [lax.dynamic_index_in_dim(cols, orb ^ m, 0, keepdims=True) for m in orb_masks]
        return jnp.concatenate(parts, axis=0)[None]

    occ_near = gather(relative(occ_cols), "pts", outer, 0)
    occ_far = swap(occ_near, "pts", last)
    vir_near = gather(relative(vir_cols), "pts", outer, 0)
    vir_far = swap(vir_near, "pts", last)
    blocks = vir_near.shape[0]

    def green(points, cols, weight):
        value = contract(weighted(cols, weight), points)
        value = value.reshape(orbs, 2, blocks, block, rows)
        return scatter_sum(value, "orb", orb_bits)[0]

    def spectral(occ, vir):
        response = -(occ * vir)
        parts = [table[k, 0] * response[0] + table[k, 1] * response[1] for k in range(2)]
        value = jnp.stack(parts, axis=1)[:, :, None]
        value = gather(value, "orb", orb_bits, 2)
        return value.reshape(-1, rows)

    occ_near_green = green(occ_points, occ_near, occ_weight)
    occ_far_green = green(occ_points, occ_far, occ_weight)
    vir_near_green = green(vir_points, vir_near, vir_weight)
    vir_far_green = green(vir_points, vir_far, vir_weight)
    spec_far = spectral(occ_far_green, vir_far_green)
    spec_near = spectral(occ_near_green, vir_near_green)

    waves = plane_waves.shape[0] // G_SPLIT
    pieces = [plane_waves[i * waves : (i + 1) * waves] for i in range(G_SPLIT)]
    arrived = [swap(contract(spec_far, piece), "pts", last) for piece in pieces]
    summed = []
    for piece, other in zip(pieces, arrived):
        value = contract(spec_near, piece) + other
        value = value.reshape(blocks, 2, orbs, block, waves)
        summed.append(scatter_sum(value, "pts", outer)[0])
    summed = jnp.concatenate(summed, axis=-1)

    def place(owner):
        apart = orb ^ owner
        width = len(orb_bits)
        return sum(((apart >> i) & 1) << (width - 1 - i) for i in range(width))

    ordered = jnp.stack(
        [lax.dynamic_index_in_dim(summed, place(o), 1, keepdims=False) for o in range(orbs)], axis=1
    )
    return jnp.transpose(ordered.reshape(2, orbs * block, -1), (0, 2, 1))


def solution(mesh):
    in_specs = (
        P("pts", "orb"),
        P("pts", "orb"),
        P("pts", "orb"),
        P("pts", "orb"),
        P("orb"),
        P("orb"),
        P("orb", "pts"),
    )
    out_specs = P(None, "orb", "pts")
    return jax.shard_map(
        on_device, mesh=mesh, in_specs=in_specs, out_specs=out_specs, check_vma=False
    )
```

time: 451 us -> 281 us (0.62)
  waiting for transfers between devices: 286 us -> 173 us
  matrix products: 101 us -> 53.9 us
  blocking collectives: 32.9 us -> 0 us
  starting transfers between devices: 0.2 us -> 29 us
  between operations: 14.2 us -> 0.43 us
  other arithmetic: 4.39 us -> 14.3 us
    ppermute x0 -> x24, waiting for transfers between devices: none -> 173 us  [swap(): lax.ppermute(x, axis, [(i, i ^ bit) for i in range(lax.axis_size(axis))])]
    all_gather x4 -> x0, waiting for transfers between devices: 104 us -> none  [the longest x1 41.7 us: on_device(): lax.all_gather(occ_points, 'orb', axis=1, tiled=True)]
    unnamed x7 -> x0, waiting for transfers between devices: 92.9 us -> none
    reduce_scatter x1 -> x0, waiting for transfers between devices: 88.6 us -> none  [on_device(): lax.psum_scatter(partial_value, 'pts', scatter_dimension=2, tiled=True)]
    dot_general x2 -> x0, matrix products: 46.2 us -> none  [the longest x1 38.3 us: on_device(): jnp.dot(plane_waves, spectral.reshape(row_count, 2 * columns), precision=...]
    all_gather x1 -> x0, blocking collectives: 32.9 us -> none  [on_device(): lax.all_gather(occ_cols, 'pts', axis=0, tiled=True)]
    ppermute x0 -> x24, starting transfers between devices: none -> 29 us  [swap(): lax.ppermute(x, axis, [(i, i ^ bit) for i in range(lax.axis_size(axis))])]
    add x0 -> x8, other arithmetic: none -> 8.92 us  [the longest x2 5.29 us: spectral(): table[k, 0] * response[0] + table[k, 1] * response[1]]
  transfers between devices with their start and end apart: 6 -> 24, of which waited for: 5 -> 15; matrix products, arithmetic and copies ran while one was open for 15% -> 26% of each run, Pallas kernels for 0% -> 0%
where the time goes in v1:
time: 281 us
  waiting for transfers between devices  173 us (62%)
  matrix products  53.9 us (19%)
  starting transfers between devices  29 us (10%)
  other arithmetic  14.3 us (5%)
  local copies, waits for them, and re-layouts  9.86 us (4%)
    ppermute x24, waiting for transfers between devices, swap(): lax.ppermute(x, axis, [(i, i ^ bit) for i in range(lax.axis_size(axis))])  173 us
    dot_general x8, matrix products, contract(): lax.dot_general(left, right, (((1,), (1,)), ((), ())), precision=lax.Prec...  53.9 us
    ppermute x24, starting transfers between devices, swap(): lax.ppermute(x, axis, [(i, i ^ bit) for i in range(lax.axis_size(axis))])  29 us
  transfers between devices with their start and end apart: 24, of which 15 were waited for; matrix products, arithmetic and copies ran while one was open for 26% of the time, Pallas kernels for 0%

profile of v1, /device:TPU:0, one launch (start us, length us, event | category | flops | bytes accessed | tf_op | source)
XLA Modules:
  0.0 280.5 jit_solution(5171604818363237335)
XLA Ops:
  0.0 0.9 constant_dynamic-slice_fusion.7
  0.9 4.1 %collective-permute-start = (f32[1,4,8,256]{3,2,1,0:T(8,128)S(1)}, f32[1,4,8,256]{3,2,1,0:T(8,128)S(1)}, u32[]{:S(2)}, u32[]{:S(2)}) collective-permute-start(f32[1,4,8,256]{3,2,1,0:T(8,128)S(1)} %maximum_bitcast_fusion.4), channel_id=1, source_target_pairs={{0,16},{4,20},{8,24},{12,28},{16,0},{20,4},{24,8},{28,12},{1,17},{... | collective-permute-start | bytes 98312 | tf_op jit(solution)/shard_map/ppermute | solution.py:30
  5.0 1.0 constant_dynamic-slice_fusion.3
  6.1 0.8 multiply_exponential_fusion
  6.9 0.3 collective-permute-done
  7.2 7.0 %collective-permute-start.1 = (f32[2,4,8,256]{3,2,1,0:T(8,128)S(1)}, f32[2,4,8,256]{3,2,1,0:T(8,128)S(1)}, u32[]{:S(2)}, u32[]{:S(2)}) collective-permute-start(f32[2,4,8,256]{3,2,1,0:T(8,128)S(1)} %pad_maximum_fusion.7), channel_id=1, source_target_pairs={{0,8},{4,12},{8,0},{12,4},{16,24},{20,28},{24,16},{28,20},{1,9},{5... | collective-permute-start | bytes 196616 | tf_op jit(solution)/shard_map/ppermute | solution.py:30
  14.3 0.8 multiply_exponential_fusion.1
  15.0 1.8 collective-permute-done.1
  16.9 1.4 collective-permute-start.10
  18.3 3.5 %collective-permute-done.4 = f32[1,4,8,2304]{3,2,1,0:T(8,128)S(1)} collective-permute-done((f32[1,4,8,2304]{3,2,1,0:T(8,128)S(1)}, f32[1,4,8,2304]{3,2,1,0:T(8,128)S(1)}, u32[]{:S(2)}, u32[]{:S(2)}) %collective-permute-start.4) | collective-permute-done | bytes 294944 | tf_op jit(solution)/shard_map/ppermute | solution.py:30
  22.0 1.4 fusion.35
  23.3 12.7 %collective-permute-done.5 = f32[2,4,8,2304]{3,2,1,0:T(8,128)S(1)} collective-permute-done((f32[2,4,8,2304]{3,2,1,0:T(8,128)S(1)}, f32[2,4,8,2304]{3,2,1,0:T(8,128)S(1)}, u32[]{:S(2)}, u32[]{:S(2)}) %collective-permute-start.5) | collective-permute-done | bytes 589856 | tf_op jit(solution)/shard_map/ppermute | solution.py:30
  36.2 1.6 collective-permute-start.13
  37.8 1.2 fusion.28
  39.0 1.4 fusion.33
  40.6 0.6 collective-permute-start.2
  41.1 21.1 %collective-permute-done.13 = f32[4,4,8,2304]{3,2,1,0:T(8,128)S(1)} collective-permute-done((f32[4,4,8,2304]{3,2,1,0:T(8,128)S(1)}, f32[4,4,8,2304]{3,2,1,0:T(8,128)S(1)}, u32[]{:S(2)}, u32[]{:S(2)}) %collective-permute-start.13) | collective-permute-done | bytes 1179680 | tf_op jit(solution)/shard_map/ppermute | solution.py:30
  62.2 0.5 broadcast_multiply_fusion.1
  62.7 13.7 %fusion.36 = f32[256,2560]{1,0:T(8,128)S(1)} fusion(f32[256,2304]{1,0:T(8,128)S(1)} %bitcast.81, f32[2560,2304]{1,0:T(8,128)} %param.12), kind=kOutput, calls=%fused_computation.78 | convolution fusion | flops 9059696640 | bytes 28573696 | tf_op jit(solution)/shard_map/dot_general | solution.py:20
  76.4 1.3 fusion.29
  77.7 13.9 %fusion.34 = f32[256,2560]{1,0:T(8,128)S(1)} fusion(f32[256,2304]{1,0:T(8,128)S(1)} %bitcast.80, f32[2560,2304]{1,0:T(8,128)} %param.12), kind=kOutput, calls=%fused_computation.76 | convolution fusion | flops 9059696640 | bytes 28573696 | tf_op jit(solution)/shard_map/dot_general | solution.py:20
  91.8 0.6 collective-permute-start.6
  92.4 1.5 add.153
  93.9 1.6 collective-permute-start.12
  95.5 0.2 add.155
  95.8 1.0 collective-permute-start.15
  96.8 0.7 fusion.32
  97.5 1.6 add.145
  99.2 1.2 collective-permute-start.3
  100.4 0.2 add.147
  100.6 1.0 collective-permute-start.7
  101.6 10.0 %collective-permute-done.12 = f32[1,2,4,8,2560]{4,3,2,1,0:T(8,128)S(1)} collective-permute-done((f32[1,2,4,8,2560]{4,3,2,1,0:T(8,128)S(1)}, f32[1,2,4,8,2560]{4,3,2,1,0:T(8,128)S(1)}, u32[]{:S(2)}, u32[]{:S(2)}) %collective-permute-start.12) | collective-permute-done | bytes 655392 | tf_op jit(solution)/shard_map/ppermute | solution.py:30
  111.5 14.0 %collective-permute-done.15 = f32[1,2,4,8,2560]{4,3,2,1,0:T(8,128)S(1)} collective-permute-done((f32[1,2,4,8,2560]{4,3,2,1,0:T(8,128)S(1)}, f32[1,2,4,8,2560]{4,3,2,1,0:T(8,128)S(1)}, u32[]{:S(2)}, u32[]{:S(2)}) %collective-permute-start.15) | collective-permute-done | bytes 655392 | tf_op jit(solution)/shard_map/ppermute | solution.py:30
  125.7 2.6 add_bitcast_fusion.1
  128.4 1.6 collective-permute-start.16
  130.0 9.6 %collective-permute-done.3 = f32[1,2,4,8,2560]{4,3,2,1,0:T(8,128)S(1)} collective-permute-done((f32[1,2,4,8,2560]{4,3,2,1,0:T(8,128)S(1)}, f32[1,2,4,8,2560]{4,3,2,1,0:T(8,128)S(1)}, u32[]{:S(2)}, u32[]{:S(2)}) %collective-permute-start.3) | collective-permute-done | bytes 655392 | tf_op jit(solution)/shard_map/ppermute | solution.py:30
  139.6 14.0 %collective-permute-done.7 = f32[1,2,4,8,2560]{4,3,2,1,0:T(8,128)S(1)} collective-permute-done((f32[1,2,4,8,2560]{4,3,2,1,0:T(8,128)S(1)}, f32[1,2,4,8,2560]{4,3,2,1,0:T(8,128)S(1)}, u32[]{:S(2)}, u32[]{:S(2)}) %collective-permute-start.7) | collective-permute-done | bytes 655392 | tf_op jit(solution)/shard_map/ppermute | solution.py:30
  153.7 0.2 fusion.17
  153.9 2.6 add_bitcast_fusion.3
  156.5 10.3 %collective-permute-done.16 = f32[4,2,1,8,2560]{4,3,0,1,2:T(8,128)S(1)} collective-permute-done((f32[4,2,1,8,2560]{4,3,0,1,2:T(8,128)S(1)}, f32[4,2,1,8,2560]{4,3,0,1,2:T(8,128)S(1)}, u32[]{:S(2)}, u32[]{:S(2)}) %collective-permute-start.16) | collective-permute-done | bytes 655392 | tf_op jit(solution)/shard_map/ppermute | solution.py:30
  167.0 1.6 collective-permute-start.8
  168.6 15.6 %collective-permute-done.8 = f32[4,2,1,8,2560]{4,3,2,1,0:T(8,128)S(1)} collective-permute-done((f32[4,2,1,8,2560]{4,3,2,1,0:T(8,128)S(1)}, f32[4,2,1,8,2560]{4,3,2,1,0:T(8,128)S(1)}, u32[]{:S(2)}, u32[]{:S(2)}) %collective-permute-start.8) | collective-permute-done | bytes 655392 | tf_op jit(solution)/shard_map/ppermute | solution.py:30
  184.4 0.2 pad_maximum_fusion.1
  184.6 0.2 copy.21
  184.9 1.6 slice-done.4
  186.5 5.9 %fusion = f32[256,1024]{1,0:T(8,128)} fusion(f32[256,2560]{1,0:T(8,128)S(1)} %bitcast.76, f32[2048,2560]{1,0:T(8,128)S(1)} %bitcast.75), kind=kOutput, calls=%fused_computation | convolution fusion | flops 4026531840 | bytes 14155776 | tf_op jit(solution)/shard_map/dot_general | solution.py:20
  192.4 1.5 collective-permute-start.21
  193.9 5.2 %fusion.4 = f32[256,1024]{1,0:T(8,128)S(1)} fusion(f32[256,2560]{1,0:T(8,128)S(1)} %bitcast.77, f32[2048,2560]{1,0:T(8,128)S(1)} %bitcast.75), kind=kOutput, calls=%fused_computation.4 | convolution fusion | flops 4026531840 | bytes 14155776 | tf_op jit(solution)/shard_map/dot_general | solution.py:20
  199.2 0.6 collective-permute-start.18
  199.8 0.2 pad_maximum_fusion
  200.0 18.8 %collective-permute-done.21 = f32[256,1024]{1,0:T(8,128)} collective-permute-done((f32[256,1024]{1,0:T(8,128)}, f32[256,1024]{1,0:T(8,128)}, u32[]{:S(2)}, u32[]{:S(2)}) %collective-permute-start.21) | collective-permute-done | bytes 1048608 | tf_op jit(solution)/shard_map/ppermute | solution.py:30
  218.8 6.2 %fusion.11 = f32[256,1024]{1,0:T(8,128)S(1)} fusion(f32[256,1024]{1,0:T(8,128)} %collective-permute-done.21, f32[256,2560]{1,0:T(8,128)S(1)} %bitcast.78, f32[2048,2560]{1,0:T(8,128)S(1)} %bitcast.75), kind=kOutput, calls=%fused_computation.13 | convolution fusion | flops 4026793984 | bytes 15204352 | tf_op jit(solution)/shard_map/dot_general | solution.py:20
  225.1 0.6 collective-permute-start.22
  225.8 14.2 %collective-permute-done.18 = f32[256,1024]{1,0:T(8,128)} collective-permute-done((f32[256,1024]{1,0:T(8,128)S(1)}, f32[256,1024]{1,0:T(8,128)}, u32[]{:S(2)}, u32[]{:S(2)}) %collective-permute-start.18) | collective-permute-done | bytes 1048608 | tf_op jit(solution)/shard_map/ppermute | solution.py:30
  240.0 6.2 %fusion.8 = f32[256,1024]{1,0:T(8,128)S(1)} fusion(f32[256,1024]{1,0:T(8,128)} %collective-permute-done.18, f32[256,2560]{1,0:T(8,128)S(1)} %bitcast.79, f32[2048,2560]{1,0:T(8,128)S(1)} %bitcast.75), kind=kOutput, calls=%fused_computation.12 | convolution fusion | flops 4026793984 | bytes 15204352 | tf_op jit(solution)/shard_map/dot_general | solution.py:20
  246.3 0.6 collective-permute-start.19
  247.0 0.7 slice.223
  247.7 2.1 collective-permute-start.23
  249.8 14.8 %collective-permute-done.19 = f32[2,2,4,8,1024]{4,3,2,1,0:T(8,128)S(1)} collective-permute-done((f32[2,2,4,8,1024]{4,3,2,1,0:T(8,128)S(1)}, f32[2,2,4,8,1024]{4,3,2,1,0:T(8,128)S(1)}, u32[]{:S(2)}, u32[]{:S(2)}) %collective-permute-start.19) | collective-permute-done | bytes 524320 | tf_op jit(solution)/shard_map/ppermute | solution.py:30
  264.7 0.8 copy-done.2
  265.5 0.7 slice.219
  266.4 12.2 %collective-permute-done.20 = f32[1,2,4,8,1024]{4,3,2,1,0:T(8,128)} collective-permute-done((f32[1,2,4,8,1024]{4,3,2,1,0:T(8,128)}, f32[1,2,4,8,1024]{4,3,2,1,0:T(8,128)}, u32[]{:S(2)}, u32[]{:S(2)}) %collective-permute-start.20) | collective-permute-done | bytes 262176 | tf_op jit(solution)/shard_map/ppermute | solution.py:30
  278.6 1.1 fusion.19
  279.7 0.8 maximum_bitcast_fusion.2
  (62 shorter events, 2.3 us)
Async XLA Ops:
  0.0 22.0 %copy-start = (f32[2560,256]{1,0:T(8,128)S(1)}, f32[2560,256]{1,0:T(8,128)}, u32[]{:S(2)}) copy-start(f32[2560,256]{1,0:T(8,128)} %param.11) | copy-start | bytes 7864324
  0.9 6.3 %collective-permute-start = (f32[1,4,8,256]{3,2,1,0:T(8,128)S(1)}, f32[1,4,8,256]{3,2,1,0:T(8,128)S(1)}, u32[]{:S(2)}, u32[]{:S(2)}) collective-permute-start(f32[1,4,8,256]{3,2,1,0:T(8,128)S(1)} %maximum_bitcast_fusion.4), channel_id=1, source_target_pairs={{0,16},{4,20},{8,24},{12,28},{16,0},{20,4},{24,8},{28,12},{1,17},{... | collective-permute-start | bytes 98312 | tf_op jit(solution)/shard_map/ppermute | solution.py:30
  6.0 15.8 %collective-permute-start.4 = (f32[1,4,8,2304]{3,2,1,0:T(8,128)S(1)}, f32[1,4,8,2304]{3,2,1,0:T(8,128)S(1)}, u32[]{:S(2)}, u32[]{:S(2)}) collective-permute-start(f32[1,4,8,2304]{3,2,1,0:T(8,128)S(1)} %maximum_bitcast_fusion.3), channel_id=1, source_target_pairs={{0,16},{4,20},{8,24},{12,28},{16,0},{20,4},{24,8},{28,12},{1,17},{... | collective-permute-start | bytes 884744 | tf_op jit(solution)/shard_map/ppermute | solution.py:30
  7.2 9.6 %collective-permute-start.1 = (f32[2,4,8,256]{3,2,1,0:T(8,128)S(1)}, f32[2,4,8,256]{3,2,1,0:T(8,128)S(1)}, u32[]{:S(2)}, u32[]{:S(2)}) collective-permute-start(f32[2,4,8,256]{3,2,1,0:T(8,128)S(1)} %pad_maximum_fusion.7), channel_id=1, source_target_pairs={{0,8},{4,12},{8,0},{12,4},{16,24},{20,28},{24,16},{28,20},{1,9},{5... | collective-permute-start | bytes 196616 | tf_op jit(solution)/shard_map/ppermute | solution.py:30
  16.9 5.0 %collective-permute-start.10 = (f32[4,4,8,256]{3,2,1,0:T(8,128)S(1)}, f32[4,4,8,256]{3,2,1,0:T(8,128)S(1)}, u32[]{:S(2)}, u32[]{:S(2)}) collective-permute-start(f32[4,4,8,256]{3,2,1,0:T(8,128)S(1)} %get-tuple-element.32), channel_id=1, source_target_pairs={{0,4},{4,0},{8,12},{12,8},{16,20},{20,16},{24,28},{28,24},{1,5},{5... | collective-permute-start | bytes 393224 | tf_op jit(solution)/shard_map/ppermute | solution.py:30
  21.8 14.2 %collective-permute-start.5 = (f32[2,4,8,2304]{3,2,1,0:T(8,128)S(1)}, f32[2,4,8,2304]{3,2,1,0:T(8,128)S(1)}, u32[]{:S(2)}, u32[]{:S(2)}) collective-permute-start(f32[2,4,8,2304]{3,2,1,0:T(8,128)S(1)} %pad_maximum_fusion.5), channel_id=1, source_target_pairs={{0,8},{4,12},{8,0},{12,4},{16,24},{20,28},{24,16},{28,20},{1,9},{5... | collective-permute-start | bytes 1769480 | tf_op jit(solution)/shard_map/ppermute | solution.py:30
  36.2 26.0 %collective-permute-start.13 = (f32[4,4,8,2304]{3,2,1,0:T(8,128)S(1)}, f32[4,4,8,2304]{3,2,1,0:T(8,128)S(1)}, u32[]{:S(2)}, u32[]{:S(2)}) collective-permute-start(f32[4,4,8,2304]{3,2,1,0:T(8,128)S(1)} %get-tuple-element.14), channel_id=1, source_target_pairs={{0,4},{4,0},{8,12},{12,8},{16,20},{20,16},{24,28},{28,24},{1,5},{5... | collective-permute-start | bytes 3538952 | tf_op jit(solution)/shard_map/ppermute | solution.py:30
  39.0 53.3 %collective-permute-start.11 = (f32[2,2,4,8,2560]{4,3,2,1,0:T(8,128)}, f32[2,2,4,8,2560]{4,3,2,1,0:T(8,128)}, u32[]{:S(2)}, u32[]{:S(2)}) collective-permute-start(f32[2,2,4,8,2560]{4,3,2,1,0:T(8,128)} %bitcast.24), channel_id=1, source_target_pairs={{0,1},{1,0},{2,3},{3,2},{4,5},{5,4},{6,7},{7,6},{8,9},{9,8},{10,11... | collective-permute-start | bytes 3932168 | tf_op jit(solution)/shard_map/ppermute | solution.py:30
  40.6 56.9 %collective-permute-start.2 = (f32[2,2,4,8,2560]{4,3,2,1,0:T(8,128)S(1)}, f32[2,2,4,8,2560]{4,3,2,1,0:T(8,128)}, u32[]{:S(2)}, u32[]{:S(2)}) collective-permute-start(f32[2,2,4,8,2560]{4,3,2,1,0:T(8,128)S(1)} %bitcast.88), channel_id=1, source_target_pairs={{0,1},{1,0},{2,3},{3,2},{4,5},{5,4},{6,7},{7,6},{8,9},{9,8},{10,11... | collective-permute-start | bytes 3932168 | tf_op jit(solution)/shard_map/ppermute | solution.py:30
  91.6 3.9 %collective-permute-start.14 = (f32[2,2,4,8,2560]{4,3,2,1,0:T(8,128)}, f32[2,2,4,8,2560]{4,3,2,1,0:T(8,128)S(1)}, u32[]{:S(2)}, u32[]{:S(2)}) collective-permute-start(f32[2,2,4,8,2560]{4,3,2,1,0:T(8,128)} %bitcast.28), channel_id=1, source_target_pairs={{0,1},{1,0},{2,3},{3,2},{4,5},{5,4},{6,7},{7,6},{8,9},{9,8},{10,11... | collective-permute-start | bytes 3932168 | tf_op jit(solution)/shard_map/ppermute | solution.py:30
  91.8 8.6 %collective-permute-start.6 = (f32[2,2,4,8,2560]{4,3,2,1,0:T(8,128)S(1)}, f32[2,2,4,8,2560]{4,3,2,1,0:T(8,128)S(1)}, u32[]{:S(2)}, u32[]{:S(2)}) collective-permute-start(f32[2,2,4,8,2560]{4,3,2,1,0:T(8,128)S(1)} %bitcast.89), channel_id=1, source_target_pairs={{0,1},{1,0},{2,3},{3,2},{4,5},{5,4},{6,7},{7,6},{8,9},{9,8},{10,11... | collective-permute-start | bytes 3932168 | tf_op jit(solution)/shard_map/ppermute | solution.py:30
  93.9 17.7 %collective-permute-start.12 = (f32[1,2,4,8,2560]{4,3,2,1,0:T(8,128)S(1)}, f32[1,2,4,8,2560]{4,3,2,1,0:T(8,128)S(1)}, u32[]{:S(2)}, u32[]{:S(2)}) collective-permute-start(f32[1,2,4,8,2560]{4,3,2,1,0:T(8,128)S(1)} %slice.209), channel_id=1, source_target_pairs={{0,2},{1,3},{2,0},{3,1},{4,6},{5,7},{6,4},{7,5},{8,10},{9,11},{10,... | collective-permute-start | bytes 1966088 | tf_op jit(solution)/shard_map/ppermute | solution.py:30
  95.5 1.2 copy-start.3
  95.5 1.2 copy-start.4
  95.5 1.2 copy-start.5
  95.8 29.8 %collective-permute-start.15 = (f32[1,2,4,8,2560]{4,3,2,1,0:T(8,128)S(1)}, f32[1,2,4,8,2560]{4,3,2,1,0:T(8,128)S(1)}, u32[]{:S(2)}, u32[]{:S(2)}) collective-permute-start(f32[1,2,4,8,2560]{4,3,2,1,0:T(8,128)S(1)} %slice.213), channel_id=1, source_target_pairs={{0,2},{1,3},{2,0},{3,1},{4,6},{5,7},{6,4},{7,5},{8,10},{9,11},{10,... | collective-permute-start | bytes 1966088 | tf_op jit(solution)/shard_map/ppermute | solution.py:30
  97.5 87.4 %slice-start = ((s8[20971520]{0:T(1024)(128)(4,1)}), s8[4194304]{0:T(1024)(128)(4,1)S(1)}, s32[]{:S(2)}) async-start(s8[20971520]{0:T(1024)(128)(4,1)} %bitcast.74), calls=%async_computation | async-start | bytes 8388608
  99.2 40.5 %collective-permute-start.3 = (f32[1,2,4,8,2560]{4,3,2,1,0:T(8,128)S(1)}, f32[1,2,4,8,2560]{4,3,2,1,0:T(8,128)S(1)}, u32[]{:S(2)}, u32[]{:S(2)}) collective-permute-start(f32[1,2,4,8,2560]{4,3,2,1,0:T(8,128)S(1)} %slice.199), channel_id=1, source_target_pairs={{0,2},{1,3},{2,0},{3,1},{4,6},{5,7},{6,4},{7,5},{8,10},{9,11},{10,... | collective-permute-start | bytes 1966088 | tf_op jit(solution)/shard_map/ppermute | solution.py:30
  100.4 84.5 %slice-start.1 = ((s8[20971520]{0:T(1024)(128)(4,1)}), s8[4194304]{0:T(1024)(128)(4,1)S(1)}, s32[]{:S(2)}) async-start(s8[20971520]{0:T(1024)(128)(4,1)} %bitcast.74), calls=%async_computation.1 | async-start | bytes 8388608
  100.6 53.1 %collective-permute-start.7 = (f32[1,2,4,8,2560]{4,3,2,1,0:T(8,128)S(1)}, f32[1,2,4,8,2560]{4,3,2,1,0:T(8,128)S(1)}, u32[]{:S(2)}, u32[]{:S(2)}) collective-permute-start(f32[1,2,4,8,2560]{4,3,2,1,0:T(8,128)S(1)} %slice.203), channel_id=1, source_target_pairs={{0,2},{1,3},{2,0},{3,1},{4,6},{5,7},{6,4},{7,5},{8,10},{9,11},{10,... | collective-permute-start | bytes 1966088 | tf_op jit(solution)/shard_map/ppermute | solution.py:30
  128.4 56.5 %slice-start.2 = ((s8[20971520]{0:T(1024)(128)(4,1)}), s8[4194304]{0:T(1024)(128)(4,1)S(1)}, s32[]{:S(2)}) async-start(s8[20971520]{0:T(1024)(128)(4,1)} %bitcast.74), calls=%async_computation.2 | async-start | bytes 8388608
  128.4 38.3 %collective-permute-start.16 = (f32[4,2,1,8,2560]{4,3,0,1,2:T(8,128)S(1)}, f32[4,2,1,8,2560]{4,3,0,1,2:T(8,128)S(1)}, u32[]{:S(2)}, u32[]{:S(2)}) collective-permute-start(f32[4,2,1,8,2560]{4,3,0,1,2:T(8,128)S(1)} %maximum_bitcast_fusion.1), channel_id=1, source_target_pairs={{0,2},{1,3},{2,0},{3,1},{4,6},{5,7},{6,4},{7,5},{8,10},{9,11},{10,... | collective-permute-start | bytes 1966088 | tf_op jit(solution)/shard_map/ppermute | solution.py:30
  156.5 28.4 %slice-start.3 = ((s8[20971520]{0:T(1024)(128)(4,1)}), s8[4194304]{0:T(1024)(128)(4,1)S(1)}, s32[]{:S(2)}) async-start(s8[20971520]{0:T(1024)(128)(4,1)} %bitcast.74), calls=%async_computation.3 | async-start | bytes 8388608
  166.9 17.5 %collective-permute-start.17 = (f32[4,2,2,8,2560]{4,3,0,1,2:T(8,128)S(1)}, f32[4,2,2,8,2560]{4,3,0,1,2:T(8,128)S(1)}, u32[]{:S(2)}, u32[]{:S(2)}) collective-permute-start(f32[4,2,2,8,2560]{4,3,0,1,2:T(8,128)S(1)} %pad_maximum_fusion.3), channel_id=1, source_target_pairs={{0,1},{1,0},{2,3},{3,2},{4,5},{5,4},{6,7},{7,6},{8,9},{9,8},{10,11... | collective-permute-start | bytes 3932168 | tf_op jit(solution)/shard_map/ppermute | solution.py:30
  167.0 17.2 %collective-permute-start.8 = (f32[4,2,1,8,2560]{4,3,2,1,0:T(8,128)S(1)}, f32[4,2,1,8,2560]{4,3,2,1,0:T(8,128)S(1)}, u32[]{:S(2)}, u32[]{:S(2)}) collective-permute-start(f32[4,2,1,8,2560]{4,3,2,1,0:T(8,128)S(1)} %maximum_bitcast_fusion), channel_id=1, source_target_pairs={{0,2},{1,3},{2,0},{3,1},{4,6},{5,7},{6,4},{7,5},{8,10},{9,11},{10,... | collective-permute-start | bytes 1966088 | tf_op jit(solution)/shard_map/ppermute | solution.py:30
  184.3 2.2 slice-start.4
  184.3 15.4 %collective-permute-start.9 = (f32[4,2,2,8,2560]{4,3,2,1,0:T(8,128)S(1)}, f32[4,2,2,8,2560]{4,3,2,1,0:T(8,128)S(1)}, u32[]{:S(2)}, u32[]{:S(2)}) collective-permute-start(f32[4,2,2,8,2560]{4,3,2,1,0:T(8,128)S(1)} %pad_maximum_fusion.2), channel_id=1, source_target_pairs={{0,1},{1,0},{2,3},{3,2},{4,5},{5,4},{6,7},{7,6},{8,9},{9,8},{10,11... | collective-permute-start | bytes 3932168 | tf_op jit(solution)/shard_map/ppermute | solution.py:30
  192.4 26.4 %collective-permute-start.21 = (f32[256,1024]{1,0:T(8,128)}, f32[256,1024]{1,0:T(8,128)}, u32[]{:S(2)}, u32[]{:S(2)}) collective-permute-start(f32[256,1024]{1,0:T(8,128)} %fusion), channel_id=1, source_target_pairs={{0,4},{4,0},{8,12},{12,8},{16,20},{20,16},{24,28},{28,24},{1,5},{5... | collective-permute-start | bytes 3145736 | tf_op jit(solution)/shard_map/ppermute | solution.py:30
  199.2 40.8 %collective-permute-start.18 = (f32[256,1024]{1,0:T(8,128)S(1)}, f32[256,1024]{1,0:T(8,128)}, u32[]{:S(2)}, u32[]{:S(2)}) collective-permute-start(f32[256,1024]{1,0:T(8,128)S(1)} %fusion.4), channel_id=1, source_target_pairs={{0,4},{4,0},{8,12},{12,8},{16,20},{20,16},{24,28},{28,24},{1,5},{5... | collective-permute-start | bytes 3145736 | tf_op jit(solution)/shard_map/ppermute | solution.py:30
  225.1 21.8 %collective-permute-start.22 = (f32[2,2,4,8,1024]{4,3,2,1,0:T(8,128)S(1)}, f32[2,2,4,8,1024]{4,3,2,1,0:T(8,128)S(1)}, u32[]{:S(2)}, u32[]{:S(2)}) collective-permute-start(f32[2,2,4,8,1024]{4,3,2,1,0:T(8,128)S(1)} %bitcast.92), channel_id=1, source_target_pairs={{0,8},{4,12},{8,0},{12,4},{16,24},{20,28},{24,16},{28,20},{1,9},{5... | collective-permute-start | bytes 1572872 | tf_op jit(solution)/shard_map/ppermute | solution.py:30
  246.3 18.3 %collective-permute-start.19 = (f32[2,2,4,8,1024]{4,3,2,1,0:T(8,128)S(1)}, f32[2,2,4,8,1024]{4,3,2,1,0:T(8,128)S(1)}, u32[]{:S(2)}, u32[]{:S(2)}) collective-permute-start(f32[2,2,4,8,1024]{4,3,2,1,0:T(8,128)S(1)} %bitcast.93), channel_id=1, source_target_pairs={{0,8},{4,12},{8,0},{12,4},{16,24},{20,28},{24,16},{28,20},{1,9},{5... | collective-permute-start | bytes 1572872 | tf_op jit(solution)/shard_map/ppermute | solution.py:30
  247.7 18.6 %collective-permute-start.23 = (f32[1,2,4,8,1024]{4,3,2,1,0:T(8,128)}, f32[1,2,4,8,1024]{4,3,2,1,0:T(8,128)S(1)}, u32[]{:S(2)}, u32[]{:S(2)}) collective-permute-start(f32[1,2,4,8,1024]{4,3,2,1,0:T(8,128)} %slice.223), channel_id=1, source_target_pairs={{0,16},{4,20},{8,24},{12,28},{16,0},{20,4},{24,8},{28,12},{1,17},{... | collective-permute-start | bytes 786440 | tf_op jit(solution)/shard_map/ppermute | solution.py:30
  264.6 15.9 %copy-start.1 = (f32[2560,256]{1,0:T(8,128)S(1)}, f32[2560,256]{1,0:T(8,128)}, u32[]{:S(2)}) copy-start(f32[2560,256]{1,0:T(8,128)} %param.11) | copy-start | bytes 7864324
  264.7 0.8 copy-start.2
  266.2 12.4 %collective-permute-start.20 = (f32[1,2,4,8,1024]{4,3,2,1,0:T(8,128)}, f32[1,2,4,8,1024]{4,3,2,1,0:T(8,128)}, u32[]{:S(2)}, u32[]{:S(2)}) collective-permute-start(f32[1,2,4,8,1024]{4,3,2,1,0:T(8,128)} %slice.219), channel_id=1, source_target_pairs={{0,16},{4,20},{8,24},{12,28},{16,0},{20,4},{24,8},{28,12},{1,17},{... | collective-permute-start | bytes 786440 | tf_op jit(solution)/shard_map/ppermute | solution.py:30
